TPU v7x, 256 devices: a whole 4x4x8 slice. The times are simulated.
256 devices in a mesh: example: 64 (over x, z, core), feature: 4 (over y).
Axes of the slice: x: 4, y: 4, z: 8, core: 2. Of those that a mesh axis runs over, the one named last changes fastest.
Arguments:
- embeddings: bfloat16 [36864, 16384], P('example', 'feature'), may hold values from -16 to 16
- subspace: bfloat16 [16384, 128], P('feature'), may hold values from -0.046875 to 0.046875
- noise_levels: int32 [16384, 128], P('feature'), may hold values from -16 to 16
- targets: int32 [2048], replicated, may hold values from 0 to 16383
Outputs:
- embedding_grad: bfloat16 [36864, 16384], P('example', 'feature')
All inputs are finite; a program needn't handle non-finite values.
Results may differ from a plain program's by a relative error of at most 0.0085.
Values may be sent and summed in bfloat16 or wider, within the bound.
A program may use at most 64 MiB of HBM per device.

v0:
```python
import jax
import jax.numpy as jnp
from jax import lax
from jax.sharding import PartitionSpec as P

NOISE_STEP = 1.0 / 4096.0
HIGH = lax.Precision.HIGHEST


def transposed(former, latter, precision=None):
    return lax.dot_general(
        former,
        latter,
        (((0,), (0,)), ((), ())),
        precision=precision,
        preferred_element_type=jnp.float32,
    )


def by_columns(former, latter):
    return lax.dot_general(
        former, latter, (((1,), (1,)), ((), ())), preferred_element_type=jnp.float32
    )


def count_rows(targets, first, length):
    local = targets - first
    inside = (local >= 0) & (local < length)
    slots = jnp.where(inside, local, length)
    ones = jnp.ones(targets.shape, jnp.float32)
    return jax.ops.segment_sum(ones, slots, num_segments=length + 1)[:length]


def upper_factor(gram_matrix):
    return jnp.linalg.cholesky(gram_matrix).T


def factorize(gram_matrix):
    lower_factor = jnp.linalg.cholesky(gram_matrix)
    identity = jnp.eye(gram_matrix.shape[0], dtype=jnp.float32)
    inverse_factor = jax.scipy.linalg.solve_triangular(lower_factor, identity, lower=True)
    gram_inverse = jnp.dot(inverse_factor.T, inverse_factor, precision=HIGH)
    return (inverse_factor, gram_inverse)


def on_device(embeddings, subspace, noise_levels, targets):
    row_count, local_width = embeddings.shape
    examples = lax.axis_size("example")
    total_rows = row_count * examples
    projected = lax.psum(
        jnp.dot(embeddings, subspace, preferred_element_type=jnp.float32), "feature"
    )
    projected_low = projected.astype(jnp.bfloat16)
    feature_first = lax.axis_index("feature") * local_width
    share = local_width // examples
    summed = lax.psum_scatter(
        transposed(embeddings, projected_low), "example", scatter_dimension=0, tiled=True
    )
    offset = lax.axis_index("example") * share
    noise_part = lax.dynamic_slice_in_dim(noise_levels, offset, share, 0)
    image = summed / total_rows + NOISE_STEP * noise_part.astype(jnp.float32)
    row_counts = count_rows(targets, feature_first + offset, share)
    gram_matrix = lax.psum(transposed(image, image, HIGH), ("example", "feature"))
    inverse_factor, gram_inverse = factorize(gram_matrix)
    orthonormal = jnp.dot(image, inverse_factor.T, precision=HIGH)
    alignment = lax.psum(
        transposed(orthonormal * row_counts[:, None], orthonormal, HIGH), ("example", "feature")
    )
    factor_grad = 2.0 * jnp.dot(alignment, inverse_factor, precision=HIGH)
    unused, pull_back = jax.vjp(upper_factor, gram_matrix)
    gram_grad = pull_back(factor_grad)[0]
    image_grad = jnp.dot(image, gram_grad + gram_grad.T, precision=HIGH) - 2.0 * row_counts[
        :, None
    ] * jnp.dot(image, gram_inverse, precision=HIGH)
    grad_low = image_grad.astype(jnp.bfloat16)
    grad_low = lax.all_gather(grad_low, "example", axis=0, tiled=True)
    back_sum = lax.psum(
        jnp.dot(embeddings, grad_low, preferred_element_type=jnp.float32), "feature"
    )
    back_rows = back_sum.astype(jnp.bfloat16)
    result = by_columns(projected_low, grad_low) + by_columns(back_rows, subspace)
    return result.astype(jnp.bfloat16)


def solution(mesh):
    in_specs = (P("example", "feature"), P("feature", None), P("feature", None), P())
    out_specs = P("example", "feature")
    return jax.shard_map(
        on_device, mesh=mesh, in_specs=in_specs, out_specs=out_specs, check_vma=False
    )
```

profile of v0, /device:TPU:2, one launch (start us, length us, event | category | flops | bytes accessed | tf_op | source)
XLA Modules:
  0.0 797.7 jit_solution(3288870860719686440)
XLA Ops:
  6.5 4.2 fusion.45
  10.7 20.2 %all-reduce.8 = bf16[576,128]{1,0:T(8,128)(2,1)S(1)} all-reduce(f32[576,128]{1,0:T(8,128)S(1)} %fusion.45), channel_id=1, replica_groups=mesh['example'=64,'feature'=4] {'feature'}, use_global_device_ids=true, to_apply=%region_0.0 | all-reduce | flops 73728 | bytes 442368 | tf_op jit(solution)/shard_map/psum | solution.py:50
  30.9 4.7 convolution_bitcast_fusion
  35.6 2.9 copy.14
  38.8 14.7 %scatter_custom_fusion = f32[65]{0:T(128)S(1)} fusion(s32[2048]{0:T(1024)S(1)} %and_select_fusion, f32[2048]{0:T(1024)S(1)} %broadcast.95, f32[]{:T(128)} %constant.76.clone.1), kind=kCustom, calls=%fused_computation.59 | custom fusion | flops 2048 | bytes 264 | tf_op jit(solution)/shard_map/scatter-add | solution.py:31
  53.5 126.3 %reduce-scatter.4.cloned.1.call-done = f32[64,128]{1,0:T(8,128)} async-done(((f32[4096,128]{1,0:T(8,128)}), f32[64,128]{1,0:T(8,128)}) %reduce-scatter.4.cloned.1.call-update) | async-done | bytes 32784
  179.7 0.8 copy.15
  180.6 0.9 fusion.46
  181.6 240.4 %all-reduce.5.cloned.1.call-done = f32[128,128]{0,1:T(8,128)} async-done(((f32[128,128]{0,1:T(8,128)}), f32[128,128]{0,1:T(8,128)}) %all-reduce.5.cloned.1.call-update) | async-done | bytes 65552 | tf_op jit(solution)/shard_map/psum | solution.py:63
  422.0 0.9 copy.11
  423.0 0.9 fusion.22
  423.8 11.7 %custom-call.14 = f32[128,128]{1,0:T(8,128)S(1)} custom-call(f32[128,128]{1,0:T(8,128)S(1)} %fusion.22), custom_call_target="Cholesky" | custom-call | tf_op jit(solution)/shard_map/jvp(jit(cholesky))/cholesky/custom-call.1 | solution.py:35
  435.6 0.7 compare_reduce_fusion
  436.9 9.8 %custom-call.13 = f32[1,128,128]{1,2,0:T(8,128)S(1)} custom-call(f32[1,128,128]{2,1,0:T(8,128)S(1)} %fusion.24), custom_call_target="InvertDiagBlocksLowerTriangular" | custom-call | tf_op jit(solution)/shard_map/transpose(jvp(jit(cholesky)))/triangular_solve | solution.py:35
  447.2 1.0 fusion.29
  448.7 233.9 %all-reduce.7.cloned.1.call-done = f32[128,128]{1,0:T(8,128)} async-done(((f32[128,128]{1,0:T(8,128)}), f32[128,128]{1,0:T(8,128)}) %all-reduce.7.cloned.1.call-update) | async-done | bytes 65552 | tf_op jit(solution)/shard_map/psum | solution.py:66
  682.6 1.1 fusion.1
  683.7 0.9 fusion
  685.5 0.9 fusion.3
  686.4 72.9 %all-gather.2.cloned.1.call-done = bf16[4096,128]{1,0:T(8,128)(2,1)} async-done(((bf16[64,128]{1,0:T(8,128)(2,1)}), bf16[4096,128]{1,0:T(8,128)(2,1)}) %all-gather.2.cloned.1.call-update) | async-done | bytes 1048592 | tf_op jit(solution)/shard_map/all_gather | solution.py:76
  759.3 5.2 convolution_bitcast_fusion.1
  764.5 21.6 %all-reduce.9 = bf16[576,128]{0,1:T(8,128)(2,1)S(1)} all-reduce(f32[576,128]{0,1:T(8,128)} %convolution_bitcast_fusion.1), channel_id=1, replica_groups=mesh['example'=64,'feature'=4] {'feature'}, use_global_device_ids=true, to_apply=%region_7.9 | all-reduce | flops 73728 | bytes 442368 | tf_op jit(solution)/shard_map/psum | solution.py:77
  786.1 1.4 fusion.49
  787.5 3.6 add_convert_fusion
  (32 shorter events, 2.9 us)
Async XLA Ops:
  6.5 32.1 %copy-start = (s32[4096,128]{1,0:T(8,128)S(1)}, s32[4096,128]{1,0:T(8,128)}, u32[]{:S(2)}) copy-start(s32[4096,128]{1,0:T(8,128)} %param.7) | copy-start | bytes 6291460
  6.5 173.2 %reduce-scatter.4.cloned.1.call-start = ((), (), s32[]{:S(2)}) async-start(), calls=%async_computation.4 | async-start | bytes 2129920
  35.6 3.2 copy-start.3
  38.6 383.5 %all-reduce.5.cloned.1.call-start = ((), (), s32[]{:S(2)}) async-start(), calls=%async_computation.1 | async-start | bytes 131072 | tf_op jit(solution)/shard_map/psum | solution.py:63
  181.5 501.1 %all-reduce.7.cloned.1.call-start = ((), (), s32[]{:S(2)}) async-start(), calls=%async_computation.2 | async-start | bytes 131072 | tf_op jit(solution)/shard_map/psum | solution.py:66
  448.2 311.1 %all-gather.2.cloned.1.call-start = ((), (), s32[]{:S(2)}) async-start(), calls=%async_computation.3 | async-start | bytes 1064960 | tf_op jit(solution)/shard_map/all_gather | solution.py:76
  759.3 26.8 %copy-start.1 = (bf16[4096,128]{1,0:T(8,128)(2,1)S(1)}, bf16[4096,128]{1,0:T(8,128)(2,1)}, u32[]{:S(2)}) copy-start(bf16[4096,128]{1,0:T(8,128)(2,1)} %all-gather.2.cloned.1.call-done) | copy-start | bytes 3145732
  786.1 1.4 copy-start.2
Sparse Core Ops, SparseCore 0:
  38.7 140.9 reduce-scatter.3
  186.1 235.8 all-reduce.4
  448.3 234.2 all-reduce.6
  686.6 72.6 all-gather.1
where the time goes:
time: 798 us
  waiting for transfers between devices  674 us (84%)
  blocking collectives  41.8 us (5%)
  other arithmetic  38.4 us (5%)
  matrix products  25.4 us (3%)
  between operations  13.3 us (2%)
    psum x1, waiting for transfers between devices, on_device(): lax.psum(transposed(image, image, HIGH), ('example', 'feature'))  240 us
    psum x1, waiting for transfers between devices, on_device(): lax.psum(transposed(orthonormal * row_counts[:, None], orthonormal, HIGH)...  234 us
    unnamed x5, waiting for transfers between devices  126 us
    all_gather x1, waiting for transfers between devices, on_device(): grad_low = lax.all_gather(grad_low, 'example', axis=0, tiled=True)  72.9 us
    another operation x5, other arithmetic, upper_factor(): return jnp.linalg.cholesky(gram_matrix).T  22.8 us
    psum x1, blocking collectives, on_device(): lax.psum(jnp.dot(embeddings, grad_low, preferred_element_type=jnp.float32...  21.6 us
    psum x1, blocking collectives, on_device(): lax.psum(jnp.dot(embeddings, subspace, preferred_element_type=jnp.float32...  20.2 us
  transfers between devices with their start and end apart: 4, of which 4 were waited for; matrix products, arithmetic and copies ran while one was open for 2% of the time, Pallas kernels for 0%

commit v1 on v0

--- a/solution.py
+++ b/solution.py
@@ -74,8 +74,11 @@
     ] * jnp.dot(image, gram_inverse, precision=HIGH)
     grad_low = image_grad.astype(jnp.bfloat16)
     grad_low = lax.all_gather(grad_low, "example", axis=0, tiled=True)
-    back_sum = lax.psum(
-        jnp.dot(embeddings, grad_low, preferred_element_type=jnp.float32), "feature"
+    back_sum = jnp.sum(
+        lax.all_gather(
+            jnp.dot(embeddings, grad_low, preferred_element_type=jnp.float32), "feature"
+        ),
+        axis=0,
     )
     back_rows = back_sum.astype(jnp.bfloat16)
     result = by_columns(projected_low, grad_low) + by_columns(back_rows, subspace)

time: 798 us -> 805 us (level)
  blocking collectives: 41.8 us -> 20.2 us
  waiting for transfers between devices: 674 us -> 693 us
  matrix products: 25.4 us -> 33.5 us
    psum x1 -> x0, blocking collectives: 21.6 us -> none  [on_device(): lax.psum(jnp.dot(embeddings, grad_low, preferred_element_type=jnp.float32...]
    all_gather x0 -> x1, waiting for transfers between devices: none -> 19.4 us  [on_device(): lax.all_gather(jnp.dot(embeddings, grad_low, preferred_element_type=jnp.f...]
    dot_general x2, matrix products: 5.02 us -> 13.6 us  [by_columns(): lax.dot_general(former, latter, (((1,), (1,)), ((), ())), preferred_eleme...]
    unnamed x5 -> x6, waiting for transfers between devices: 126 us -> 126 us
  transfers between devices with their start and end apart: 4 -> 5, of which waited for: 4 -> 5; matrix products, arithmetic and copies ran while one was open for 2% -> 3% of each run, Pallas kernels for 0% -> 0%
where the time goes in v1:
time: 805 us
  waiting for transfers between devices  693 us (86%)
  other arithmetic  39.7 us (5%)
  matrix products  33.5 us (4%)
  blocking collectives  20.2 us (3%)
  between operations  13.3 us (2%)
    psum x1, waiting for transfers between devices, on_device(): lax.psum(transposed(image, image, HIGH), ('example', 'feature'))  240 us
    psum x1, waiting for transfers between devices, on_device(): lax.psum(transposed(orthonormal * row_counts[:, None], orthonormal, HIGH)...  234 us
    unnamed x6, waiting for transfers between devices  126 us
    all_gather x1, waiting for transfers between devices, on_device(): grad_low = lax.all_gather(grad_low, 'example', axis=0, tiled=True)  72.7 us
    another operation x5, other arithmetic, upper_factor(): return jnp.linalg.cholesky(gram_matrix).T  22.8 us
    psum x1, blocking collectives, on_device(): lax.psum(jnp.dot(embeddings, subspace, preferred_element_type=jnp.float32...  20.2 us
    all_gather x1, waiting for transfers between devices, on_device(): lax.all_gather(jnp.dot(embeddings, grad_low, preferred_element_type=jnp.f...  19.4 us
  transfers between devices with their start and end apart: 5, of which 5 were waited for; matrix products, arithmetic and copies ran while one was open for 3% of the time, Pallas kernels for 0%

profile of v1, /device:TPU:2, one launch (start us, length us, event | category | flops | bytes accessed | tf_op | source)
XLA Modules:
  0.0 804.9 jit_solution(17014639932919916655)
XLA Ops:
  6.5 4.2 fusion.45
  10.7 20.2 %all-reduce.7 = bf16[576,128]{1,0:T(8,128)(2,1)S(1)} all-reduce(f32[576,128]{1,0:T(8,128)S(1)} %fusion.45), channel_id=1, replica_groups=mesh['example'=64,'feature'=4] {'feature'}, use_global_device_ids=true, to_apply=%region_0.0 | all-reduce | flops 73728 | bytes 442368 | tf_op jit(solution)/shard_map/psum | solution.py:50
  30.9 4.7 convolution_bitcast_fusion
  35.6 2.9 copy.14
  38.8 14.7 %scatter_custom_fusion = f32[65]{0:T(128)S(1)} fusion(s32[2048]{0:T(1024)S(1)} %and_select_fusion, f32[2048]{0:T(1024)S(1)} %broadcast.95, f32[]{:T(128)} %constant.77.clone.1), kind=kCustom, calls=%fused_computation.59 | custom fusion | flops 2048 | bytes 264 | tf_op jit(solution)/shard_map/scatter-add | solution.py:31
  53.5 126.3 %reduce-scatter.4.cloned.1.call-done = f32[64,128]{1,0:T(8,128)} async-done(((f32[4096,128]{1,0:T(8,128)}), f32[64,128]{1,0:T(8,128)}) %reduce-scatter.4.cloned.1.call-update) | async-done | bytes 32784
  179.7 0.8 copy.15
  180.6 0.9 fusion.46
  181.6 240.4 %all-reduce.4.cloned.1.call-done = f32[128,128]{0,1:T(8,128)} async-done(((f32[128,128]{0,1:T(8,128)}), f32[128,128]{0,1:T(8,128)}) %all-reduce.4.cloned.1.call-update) | async-done | bytes 65552 | tf_op jit(solution)/shard_map/psum | solution.py:63
  422.0 0.9 copy.11
  423.0 0.9 fusion.22
  423.8 11.7 %custom-call.14 = f32[128,128]{1,0:T(8,128)S(1)} custom-call(f32[128,128]{1,0:T(8,128)S(1)} %fusion.22), custom_call_target="Cholesky" | custom-call | tf_op jit(solution)/shard_map/jvp(jit(cholesky))/cholesky/custom-call.1 | solution.py:35
  436.9 9.8 %custom-call.13 = f32[1,128,128]{1,2,0:T(8,128)S(1)} custom-call(f32[1,128,128]{2,1,0:T(8,128)S(1)} %fusion.24), custom_call_target="InvertDiagBlocksLowerTriangular" | custom-call | tf_op jit(solution)/shard_map/transpose(jvp(jit(cholesky)))/triangular_solve | solution.py:35
  447.2 1.0 fusion.29
  448.7 233.9 %all-reduce.6.cloned.1.call-done = f32[128,128]{1,0:T(8,128)} async-done(((f32[128,128]{1,0:T(8,128)}), f32[128,128]{1,0:T(8,128)}) %all-reduce.6.cloned.1.call-update) | async-done | bytes 65552 | tf_op jit(solution)/shard_map/psum | solution.py:66
  682.6 1.1 fusion.1
  683.7 0.9 fusion
  685.5 0.9 fusion.3
  686.5 72.7 %all-gather.4.cloned.1.call-done = bf16[4096,128]{1,0:T(8,128)(2,1)} async-done(((bf16[64,128]{1,0:T(8,128)(2,1)}), bf16[4096,128]{1,0:T(8,128)(2,1)}) %all-gather.4.cloned.1.call-update) | async-done | bytes 1048592 | tf_op jit(solution)/shard_map/all_gather | solution.py:76
  759.2 4.7 convolution_bitcast_fusion.1
  764.0 6.3 fusion.49
  770.3 19.4 %all-gather.6.cloned.1.call-done = f32[2304,128]{1,0:T(8,128)} async-done(((f32[576,128]{1,0:T(8,128)}), f32[2304,128]{1,0:T(8,128)}) %all-gather.6.cloned.1.call-update) | async-done | bytes 1179664 | tf_op jit(solution)/shard_map/all_gather | solution.py:78
  789.8 1.3 reduce_sum.9
  791.1 7.3 add_convert_fusion
  (33 shorter events, 3.6 us)
Async XLA Ops:
  6.5 32.1 %copy-start = (s32[4096,128]{1,0:T(8,128)S(1)}, s32[4096,128]{1,0:T(8,128)}, u32[]{:S(2)}) copy-start(s32[4096,128]{1,0:T(8,128)} %param.7) | copy-start | bytes 6291460
  6.5 173.2 %reduce-scatter.4.cloned.1.call-start = ((), (), s32[]{:S(2)}) async-start(), calls=%async_computation.5 | async-start | bytes 2129920
  35.6 3.2 copy-start.2
  38.6 383.5 %all-reduce.4.cloned.1.call-start = ((), (), s32[]{:S(2)}) async-start(), calls=%async_computation.1 | async-start | bytes 131072 | tf_op jit(solution)/shard_map/psum | solution.py:63
  181.5 501.1 %all-reduce.6.cloned.1.call-start = ((), (), s32[]{:S(2)}) async-start(), calls=%async_computation.2 | async-start | bytes 131072 | tf_op jit(solution)/shard_map/psum | solution.py:66
  448.2 311.0 %all-gather.4.cloned.1.call-start = ((), (), s32[]{:S(2)}) async-start(), calls=%async_computation.3 | async-start | bytes 1064960 | tf_op jit(solution)/shard_map/all_gather | solution.py:76
  686.4 103.3 %all-gather.6.cloned.1.call-start = ((), (), s32[]{:S(2)}) async-start(), calls=%async_computation.4 | async-start | bytes 1474560 | tf_op jit(solution)/shard_map/all_gather | solution.py:78
  764.0 27.1 %copy-start.1 = (bf16[4096,128]{1,0:T(8,128)(2,1)S(1)}, bf16[4096,128]{1,0:T(8,128)(2,1)}, u32[]{:S(2)}) copy-start(bf16[4096,128]{1,0:T(8,128)(2,1)} %param.6) | copy-start | bytes 3145732
Sparse Core Ops, SparseCore 0:
  38.7 140.9 reduce-scatter.3
  186.1 235.8 all-reduce.3
  448.3 234.2 all-reduce.5
  686.6 72.6 all-gather.3
  764.1 25.6 all-gather.5
